TPU v7x, 512 devices: a whole 4x4x16 slice. The times are simulated.
512 devices in a mesh: ctx: 64 (over y, z), exp: 8 (over x, core).
Axes of the slice: x: 4, y: 4, z: 16, core: 2. Of those that a mesh axis runs over, the one named last changes fastest.
Arguments:
- x_resid: bfloat16 [512, 6144], P('exp', 'ctx'), may hold values from -16 to 16
- queries: bfloat16 [512, 6144], P('ctx', 'exp'), may hold values from -5 to 5
- keys: bfloat16 [32768, 1024], P('ctx', 'exp'), may hold values from -4 to 4
- values: bfloat16 [32768, 1024], P('ctx', 'exp'), may hold values from -4 to 4
- pattern: int32 [4, 6], replicated, may hold values from 0 to 254, as said below
- global_blocks: int32 [2], replicated, may hold values from 0 to 248, as said below
- out_weight: bfloat16 [6144, 6144], P('exp', 'ctx'), may hold values from -0.875 to 0.875
- norm_gain: float32 [6144], P('ctx'), may hold values from 0.1 to 1.9
- router: bfloat16 [6144, 8], P('ctx'), may hold values from -0.078125 to 0.078125
- expert_ids: int32 [512, 2], P('exp'), may hold values from 0 to 7, as said below
- expert_slots: int32 [512, 2], P('exp'), may hold values from 0 to 19, as said below
- w_gate: bfloat16 [8, 6144, 8192], P('exp', None, 'ctx'), may hold values from -0.078125 to 0.078125
- w_up: bfloat16 [8, 6144, 8192], P('exp', None, 'ctx'), may hold values from -0.078125 to 0.078125
- w_down: bfloat16 [8, 8192, 6144], P('exp', None, 'ctx'), may hold values from -0.0625 to 0.0625
Outputs:
- layer_out: bfloat16 [512, 6144], P('exp', 'ctx')
Inputs may be any that keep to these rules, and one draw needn't show every extreme that they name: `pattern`: each row lists 3 + 3 different key blocks, none of them a global block. `global_blocks`: 2 different key blocks. `expert_ids`: each token names two different experts; among the tokens of one index of exp (aligned blocks of 64 rows) every expert is named at most 20 times, and one expert, the same in every block, exactly 20 times. `expert_slots`: within one aligned block of 64 rows, the choices that name the same expert have different slots.
All inputs are finite; a program needn't handle non-finite values.
Results may differ from a plain program's by a relative error of at most 0.01.
Values may be sent and summed in bfloat16 or wider, within the bound.
No kernel may reach another device: no remote copies, remote signals or barrier semaphores. Data moves between devices by JAX's collectives and lax.ppermute only.
A program may use at most 64 MiB of HBM per device.

v0:
```python
import jax
import jax.numpy as jnp
from jax import lax
from jax.sharding import PartitionSpec as P

D = 6144
HD = 128
BLK = 128
CAP = 20
eps = 1e-05
masked_score = -1e30


def per_device(
    x_resid,
    queries,
    keys,
    values,
    pattern,
    global_blocks,
    out_weight,
    norm_gain,
    router,
    expert_ids,
    expert_slots,
    w_gate,
    w_up,
    w_down,
):
    all_queries = lax.all_gather(queries, "ctx", axis=0, tiled=True)
    token_count = all_queries.shape[0]
    cache_length = keys.shape[0]
    groups_local = keys.shape[1] // HD
    group = all_queries.shape[1] // HD // groups_local
    query_heads = all_queries.reshape(token_count, groups_local, group, HD)
    key_heads = keys.reshape(cache_length, groups_local, HD)
    value_heads = values.reshape(cache_length, groups_local, HD)
    scores = jnp.einsum(
        "tkgd,pkd->tkgp", query_heads, key_heads, preferred_element_type=jnp.float32
    ) * HD ** (-0.5)
    local_blocks = cache_length // BLK
    block_ids = lax.axis_index("ctx") * local_blocks + jnp.arange(local_blocks, dtype=jnp.int32)
    listed = jnp.any(pattern[:, :, None] == block_ids[None, None, :], axis=1)
    anchored = jnp.any(global_blocks[:, None] == block_ids[None, :], axis=0)
    allowed_blocks = listed | anchored[None, :]
    allowed = jnp.repeat(jnp.repeat(allowed_blocks, BLK, axis=0), BLK, axis=1)[:, None, None, :]
    local_peak = jnp.max(jnp.where(allowed, scores, masked_score), axis=-1)
    peak = lax.pmax(local_peak, "ctx")
    probs = jnp.where(allowed, jnp.exp(scores - peak[..., None]), 0.0).astype(jnp.bfloat16)
    numerator = jnp.einsum("tkgp,pkd->tkgd", probs, value_heads, preferred_element_type=jnp.float32)
    denominator = jnp.sum(probs, axis=-1, dtype=jnp.float32)
    numerator, denominator = lax.psum((numerator, denominator), "ctx")
    attention = (numerator / denominator[..., None]).astype(jnp.bfloat16).reshape(token_count, -1)
    exp_count = lax.axis_size("exp")
    head_total = lax.psum_scatter(
        jnp.dot(attention, out_weight, preferred_element_type=jnp.float32),
        "exp",
        scatter_dimension=0,
        tiled=True,
    )
    residual = x_resid.astype(jnp.float32) + head_total
    scaled = residual * norm_gain
    router_wide = router.astype(jnp.float32)
    squares = lax.psum(jnp.sum(residual * residual, axis=1), "ctx")
    inverse = lax.rsqrt(squares / D + eps)
    logits = lax.psum(
        jnp.dot(scaled * inverse[:, None], router_wide, precision=lax.Precision.HIGHEST), "ctx"
    )
    normed = (scaled * inverse[:, None]).astype(jnp.bfloat16)
    experts_all = router.shape[1]
    onehot = expert_ids[:, :, None] == jnp.arange(experts_all, dtype=jnp.int32)[None, None, :]
    chosen_logits = jnp.sum(jnp.where(onehot, logits[:, None, :], 0.0), axis=-1)
    gate_weights = jax.nn.sigmoid(chosen_logits - chosen_logits[:, ::-1])
    flat_slots = expert_ids * CAP + expert_slots
    positions = jnp.arange(experts_all * CAP, dtype=jnp.int32)
    dispatch = jnp.sum(
        (flat_slots[None, :, :] == positions[:, None, None]).astype(jnp.bfloat16), axis=2
    )
    local_experts = w_gate.shape[0]
    feature_rows = lax.all_gather(normed, "ctx", axis=1, tiled=True)
    outgoing = jnp.dot(dispatch, feature_rows, preferred_element_type=jnp.float32).astype(
        jnp.bfloat16
    )
    outgoing = outgoing.reshape(experts_all, CAP, -1)
    incoming = lax.all_to_all(outgoing, "exp", split_axis=0, concat_axis=0, tiled=True)
    incoming = incoming.reshape(exp_count, local_experts, CAP, -1)
    expert_gate = jnp.einsum("sjcd,jdf->sjcf", incoming, w_gate, preferred_element_type=jnp.float32)
    expert_lift = jnp.einsum("sjcd,jdf->sjcf", incoming, w_up, preferred_element_type=jnp.float32)
    hidden = (jax.nn.silu(expert_gate) * expert_lift).astype(jnp.bfloat16)
    out_width = w_down.shape[2]
    expert_out = jnp.einsum(
        "sjcf,jfd->sjcd",
        lax.all_gather(hidden, "ctx", axis=3, tiled=True),
        w_down,
        preferred_element_type=jnp.float32,
    ).astype(jnp.bfloat16)
    returned = lax.all_to_all(
        expert_out.reshape(experts_all, CAP, out_width),
        "exp",
        split_axis=0,
        concat_axis=0,
        tiled=True,
    )
    picked = jnp.take(returned.reshape(experts_all * CAP, out_width), flat_slots, axis=0).astype(
        jnp.float32
    )
    mixture = jnp.sum(gate_weights[:, :, None] * picked, axis=1)
    return (residual + mixture).astype(jnp.bfloat16)


def solution(mesh):
    in_specs = (
        P("exp", "ctx"),
        P("ctx", "exp"),
        P("ctx", "exp"),
        P("ctx", "exp"),
        P(),
        P(),
        P("exp", "ctx"),
        P("ctx"),
        P("ctx", None),
        P("exp", None),
        P("exp", None),
        P("exp", None, "ctx"),
        P("exp", None, "ctx"),
        P("exp", None, "ctx"),
    )
    out_specs = P("exp", "ctx")
    return jax.shard_map(
        per_device, mesh=mesh, in_specs=in_specs, out_specs=out_specs, check_vma=False
    )
```

profile of v0, /device:TPU:1, one launch (start us, length us, event | category | flops | bytes accessed | tf_op | source)
XLA Modules:
  0.0 1161.9 jit_solution(5624072325766790315)
XLA Ops:
  6.5 0.0 copy-start
  6.5 0.0 all-reduce.2.cloned.1.call-start
  6.5 1.0 compare_reduce_fusion
  7.6 0.8 compare_reduce_fusion.1
  8.3 0.1 copy.41
  8.4 0.1 broadcast_bitcast_fusion
  8.5 82.7 %all_gather.9 = bf16[512,768]{1,0:T(8,128)(2,1)S(1)} all-gather(bf16[8,768]{1,0:T(8,128)(2,1)} %param.15), channel_id=1, replica_groups=mesh['ctx'=64,'exp'=8] {'ctx'}, dimensions={0}, use_global_device_ids=true | all-gather | bytes 798720 | tf_op jit(solution)/shard_map/all_gather | solution.py:30
  91.3 0.3 copy.42
  91.5 0.1 broadcast_in_dim.67
  91.6 0.0 copy-start.16
  91.6 4.8 fusion
  96.4 221.4 %pmax.7 = f32[512,6]{0,1:T(8,128)S(1)} all-reduce(f32[512,6]{0,1:T(8,128)S(1)} %get-tuple-element.7), channel_id=1, replica_groups=mesh['ctx'=64,'exp'=8] {'ctx'}, use_global_device_ids=true, to_apply=%region_3.4 | all-reduce | flops 3072 | bytes 24576 | tf_op jit(solution)/shard_map/pmax | solution.py:48
  317.8 0.0 copy-done.16
  317.8 5.6 fusion.13
  323.4 0.0 all-reduce.2.cloned.1.call-update
  323.4 0.0 reduce-scatter.2.cloned.1.call-start
  323.5 4.1 convert_reduce_fusion
  327.6 0.0 copy-start.4
  327.6 0.0 copy-start.8
  327.6 0.0 copy-start.11
  327.6 0.0 copy-start.5
  327.6 0.0 copy-start.12
  327.6 219.7 %psum.29 = f32[512,6]{0,1:T(8,128)S(1)} all-reduce(f32[512,6]{0,1:T(8,128)S(1)} %convert_reduce_fusion), channel_id=1, replica_groups=mesh['ctx'=64,'exp'=8] {'ctx'}, use_global_device_ids=true, to_apply=%region_6.7 | all-reduce | flops 3072 | bytes 24576 | tf_op jit(solution)/shard_map/psum | solution.py:52
  547.3 113.2 %all-reduce.2.cloned.1.call-done = f32[512,1,6,128]{3,0,2,1:T(8,128)} async-done(((f32[512,1,6,128]{3,0,2,1:T(8,128)}), f32[512,1,6,128]{3,0,2,1:T(8,128)}) %all-reduce.2.cloned.1.call-update) | async-done | bytes 1572880 | tf_op jit(solution)/shard_map/psum | solution.py:52
  660.5 1.9 divide_convert_fusion
  662.4 0.3 copy.45
  662.7 1.1 fusion.44
  663.8 0.0 reduce-scatter.2.cloned.1.call-update
  663.8 0.0 all-gather.3.cloned.1.call-start
  663.9 0.0 copy-done.8
  663.9 0.0 copy-done.11
  663.9 0.6 compare_and_fusion
  664.5 0.6 copy-done.6
  665.0 0.7 fusion.37
  665.7 45.5 %reduce-scatter.2.cloned.1.call-done = f32[64,96]{1,0:T(8,128)} async-done(((f32[512,96]{1,0:T(8,128)}), f32[64,96]{1,0:T(8,128)}) %reduce-scatter.2.cloned.1.call-update) | async-done | bytes 24592 | tf_op jit(solution)/shard_map/reduce_scatter | solution.py:55
  711.2 0.9 multiply_reduce_fusion.1
  712.1 115.6 %psum.30 = f32[64]{0:T(128)S(1)} all-reduce(f32[64]{0:T(128)S(1)} %multiply_reduce_fusion.1), channel_id=1, replica_groups=mesh['ctx'=64,'exp'=8] {'ctx'}, use_global_device_ids=true, to_apply=%region_9.10 | all-reduce | flops 64 | bytes 512 | tf_op jit(solution)/shard_map/psum | solution.py:64
  827.7 0.8 fusion.40
  828.5 72.3 %all-gather = bf16[64,96,64]{1,2,0:T(8,128)(2,1)S(1)} all-gather(bf16[1,96,64]{1,2,0:T(8,128)(2,1)S(1)} %fusion.40), channel_id=1, replica_groups=mesh['ctx'=64,'exp'=8] {'ctx'}, dimensions={0}, use_global_device_ids=true | all-gather | bytes 798720 | tf_op jit(solution)/shard_map/all_gather | solution.py:80
  900.8 0.7 copy.48
  901.5 2.3 reshape.108
  903.8 1.8 convolution_convert_fusion
  905.7 2.1 reshape.89
  907.8 88.6 %all_to_all.10 = bf16[8,20,6144]{2,1,0:T(8,128)(2,1)S(1)} all-to-all(bf16[8,20,6144]{2,1,0:T(8,128)(2,1)} %reshape.89), channel_id=1, replica_groups=mesh['ctx'=64,'exp'=8] {'exp'}, dimensions={0} | all-to-all | bytes 3932160 | tf_op jit(solution)/shard_map/all_to_all | solution.py:85
  996.4 0.0 copy-start.13
  996.5 0.0 copy-start.15
  996.5 0.0 copy-start.17
  996.5 0.8 fusion.16
  997.3 0.6 copy-done.1
  997.8 1.4 fusion.25
  999.2 0.0 all-gather.3.cloned.1.call-update
  999.3 0.1 copy.49
  999.4 0.1 reshape.99
  999.5 0.1 copy.47
  999.7 0.2 fusion.39
  999.9 113.2 %psum.31 = f32[64,8]{0,1:T(8,128)S(1)} all-reduce(f32[64,8]{0,1:T(8,128)S(1)} %fusion.39), channel_id=1, replica_groups=mesh['ctx'=64,'exp'=8] {'ctx'}, use_global_device_ids=true, to_apply=%region_10.11 | all-reduce | flops 512 | bytes 4096 | tf_op jit(solution)/shard_map/psum | solution.py:66
  1113.1 9.4 all-gather.3.cloned.1.call-done
  1122.6 3.5 fusion.28
  1126.1 22.9 %all-to-all-start.1 = ((bf16[8,20,96]{2,1,0:T(8,128)(2,1)}), bf16[8,20,96]{2,1,0:T(8,128)(2,1)S(1)}, u32[]{:S(2)}, u32[]{:S(2)}) async-start(bf16[8,20,96]{2,1,0:T(8,128)(2,1)} %fusion.28), calls=%async_computation.2 | async-start | bytes 98304 | tf_op jit(solution)/shard_map/all_to_all | solution.py:97
  1149.0 0.1 copy.46
  1149.1 4.7 all-to-all-done.1
  1153.8 0.7 gather_fusion
  1154.5 0.2 multiply_reduce_fusion
  1154.7 0.6 add_convert_fusion
  (31 shorter events, 0.2 us)
Async XLA Ops:
  6.5 989.9 %copy-start = (bf16[1,6144,128]{2,1,0:T(8,128)(2,1)S(1)}, bf16[1,6144,128]{2,1,0:T(8,128)(2,1)}, u32[]{:S(2)}) copy-start(bf16[1,6144,128]{2,1,0:T(8,128)(2,1)} %param.25) | copy-start | bytes 4718596
  6.5 654.0 %all-reduce.2.cloned.1.call-start = ((), (), s32[]{:S(2)}) async-start(), calls=%async_computation.3 | async-start | bytes 3145728 | tf_op jit(solution)/shard_map/psum | solution.py:52
  91.6 226.1 %copy-start.16 = (bf16[512,128]{1,0:T(8,128)(2,1)S(1)}, bf16[512,128]{1,0:T(8,128)(2,1)}, u32[]{:S(2)}) copy-start(bf16[512,128]{1,0:T(8,128)(2,1)} %param.17) | copy-start | bytes 393220
  323.4 387.8 %reduce-scatter.2.cloned.1.call-start = ((), (), s32[]{:S(2)}) async-start(), calls=%async_computation.4 | async-start | bytes 294912 | tf_op jit(solution)/shard_map/reduce_scatter | solution.py:55
  327.6 335.1 %copy-start.4 = (bf16[768,96]{0,1:T(8,128)(2,1)S(1)}, bf16[768,96]{0,1:T(8,128)(2,1)}, u32[]{:S(2)}) copy-start(bf16[768,96]{0,1:T(8,128)(2,1)} %param.20) | copy-start | bytes 442372
  327.6 336.3 %copy-start.8 = (s32[64,2]{0,1:T(2,128)S(1)}, s32[64,2]{0,1:T(2,128)}, u32[]{:S(2)}) copy-start(s32[64,2]{0,1:T(2,128)} %param.23) | copy-start | bytes 1540
  327.6 336.3 %copy-start.11 = (s32[64,2]{0,1:T(2,128)S(1)}, s32[64,2]{0,1:T(2,128)}, u32[]{:S(2)}) copy-start(s32[64,2]{0,1:T(2,128)} %param.24) | copy-start | bytes 1540
  327.6 383.6 %copy-start.5 = (bf16[64,96]{1,0:T(8,128)(2,1)S(1)}, bf16[64,96]{1,0:T(8,128)(2,1)}, u32[]{:S(2)}) copy-start(bf16[64,96]{1,0:T(8,128)(2,1)} %param.14) | copy-start | bytes 36868
  327.6 500.0 %copy-start.12 = (f32[96]{0:T(128)S(1)}, f32[96]{0:T(128)}, u32[]{:S(2)}) copy-start(f32[96]{0:T(128)} %param.21) | copy-start | bytes 1156
  663.8 458.7 %all-gather.3.cloned.1.call-start = ((), (), s32[]{:S(2)}) async-start(), calls=%async_computation.5 | async-start | bytes 3194880 | tf_op jit(solution)/shard_map/all_gather | solution.py:93
  664.5 0.6 copy-start.6
  827.7 73.8 %copy-start.14 = (f32[64]{0:T(128)}, f32[64]{0:T(128)S(1)}, u32[]{:S(2)}) copy-start(f32[64]{0:T(128)S(1)} %add_rsqrt_fusion) | copy-start | bytes 772
  996.4 1.4 copy-start.1
  996.4 2.8 copy-start.7
  996.4 3.1 copy-start.10
  996.4 3.2 copy-start.3
  996.4 3.2 copy-start.13
  996.5 3.2 copy-start.15
  996.5 3.2 copy-start.17
  997.8 115.3 %copy-start.9 = (s32[64,2]{0,1:T(2,128)S(1)}, s32[64,2]{0,1:T(2,128)}, u32[]{:S(2)}) copy-start(s32[64,2]{0,1:T(2,128)} %param.23) | copy-start | bytes 1540
  997.8 124.7 %copy-start.2 = (bf16[1,8192,96]{1,2,0:T(8,128)(2,1)S(1)}, bf16[1,8192,96]{1,2,0:T(8,128)(2,1)}, u32[]{:S(2)}) copy-start(bf16[1,8192,96]{1,2,0:T(8,128)(2,1)} %param.27) | copy-start | bytes 4718596
  1126.1 27.7 %all-to-all-start.1 = ((bf16[8,20,96]{2,1,0:T(8,128)(2,1)}), bf16[8,20,96]{2,1,0:T(8,128)(2,1)S(1)}, u32[]{:S(2)}, u32[]{:S(2)}) async-start(bf16[8,20,96]{2,1,0:T(8,128)(2,1)} %fusion.28), calls=%async_computation.2 | async-start | bytes 98304 | tf_op jit(solution)/shard_map/all_to_all | solution.py:97
Sparse Core Ops, SparseCore 0:
  323.6 336.9 all-reduce.1
  664.0 47.1 reduce-scatter.1
  999.4 123.1 all-gather.2
where the time goes:
time: 1160 us
  blocking collectives  914 us (79%)
  waiting for transfers between devices  173 us (15%)
  starting transfers between devices  23 us (2%)
  matrix products  19.2 us (2%)
  between operations  13.4 us (1%)
  other arithmetic  11.6 us (1%)
    pmax x1, blocking collectives, per_device(): peak = lax.pmax(local_peak, 'ctx')  221 us
    psum x1, blocking collectives, per_device(): numerator, denominator = lax.psum((numerator, denominator), 'ctx')  220 us
    psum x1, blocking collectives, per_device(): squares = lax.psum(jnp.sum(residual * residual, axis=1), 'ctx')  116 us
    psum x1, blocking collectives, per_device(): lax.psum(jnp.dot(scaled * inverse[:, None], router_wide, precision=lax.Pr...  113 us
    psum x1, waiting for transfers between devices, per_device(): numerator, denominator = lax.psum((numerator, denominator), 'ctx')  113 us
    all_to_all x1, blocking collectives, per_device(): lax.all_to_all(outgoing, 'exp', split_axis=0, concat_axis=0, tiled=True)  88.6 us
    all_gather x1, blocking collectives, per_device(): all_queries = lax.all_gather(queries, 'ctx', axis=0, tiled=True)  82.7 us
    all_gather x1, blocking collectives, per_device(): feature_rows = lax.all_gather(normed, 'ctx', axis=1, tiled=True)  72.3 us
  transfers between devices with their start and end apart: 4, of which 4 were waited for; matrix products, arithmetic and copies ran while one was open for 1% of the time, Pallas kernels for 0%

commit v1 on v0

--- a/solution.py
+++ b/solution.py
@@ -27,7 +27,9 @@
     w_up,
     w_down,
 ):
-    all_queries = lax.all_gather(queries, "ctx", axis=0, tiled=True)
+    all_queries = jnp.concatenate(
+        lax.all_to_all(jnp.stack(lax.psum(1, "ctx") * [queries], axis=0), "ctx", 0, 0), axis=0
+    )
     token_count = all_queries.shape[0]
     cache_length = keys.shape[0]
     groups_local = keys.shape[1] // HD

time: 1160 us -> 1120 us (0.966)
  blocking collectives: 914 us -> 831 us
  starting transfers between devices: 23 us -> 42.3 us
  waiting for transfers between devices: 173 us -> 187 us
    all_gather x1 -> x0, blocking collectives: 82.7 us -> none  [per_device(): all_queries = lax.all_gather(queries, 'ctx', axis=0, tiled=True)]
    all_to_all x0 -> x1, waiting for transfers between devices: none -> 37.9 us  [per_device(): lax.all_to_all(jnp.stack(lax.psum(1, 'ctx') * [queries], axis=0), 'ctx',...]
    psum x1, waiting for transfers between devices: 113 us -> 89.1 us  [per_device(): numerator, denominator = lax.psum((numerator, denominator), 'ctx')]
    all_to_all x0 -> x1, starting transfers between devices: none -> 19.3 us  [per_device(): lax.all_to_all(jnp.stack(lax.psum(1, 'ctx') * [queries], axis=0), 'ctx',...]
  transfers between devices with their start and end apart: 4 -> 5, of which waited for: 4 -> 5; matrix products, arithmetic and copies ran while one was open for 1% -> 1% of each run, Pallas kernels for 0% -> 0%
where the time goes in v1:
time: 1120 us; the launch traced here: 1110 us
  blocking collectives  831 us (74%)
  waiting for transfers between devices  187 us (17%)
  starting transfers between devices  42.3 us (4%)
  matrix products  18.3 us (2%)
  between operations  13.4 us (1%)
  other arithmetic  11.5 us (1%)
    pmax x1, blocking collectives, per_device(): peak = lax.pmax(local_peak, 'ctx')  222 us
    psum x1, blocking collectives, per_device(): numerator, denominator = lax.psum((numerator, denominator), 'ctx')  219 us
    psum x1, blocking collectives, per_device(): squares = lax.psum(jnp.sum(residual * residual, axis=1), 'ctx')  116 us
    psum x1, blocking collectives, per_device(): lax.psum(jnp.dot(scaled * inverse[:, None], router_wide, precision=lax.Pr...  113 us
    psum x1, waiting for transfers between devices, per_device(): numerator, denominator = lax.psum((numerator, denominator), 'ctx')  89.1 us
    all_to_all x1, blocking collectives, per_device(): lax.all_to_all(outgoing, 'exp', split_axis=0, concat_axis=0, tiled=True)  88.5 us
    all_gather x1, blocking collectives, per_device(): feature_rows = lax.all_gather(normed, 'ctx', axis=1, tiled=True)  72.4 us
    reduce_scatter x1, waiting for transfers between devices, per_device(): lax.psum_scatter(jnp.dot(attention, out_weight, preferred_element_type=jn...  45.7 us
  transfers between devices with their start and end apart: 5, of which 5 were waited for; matrix products, arithmetic and copies ran while one was open for 1% of the time, Pallas kernels for 0%

profile of v1, /device:TPU:1, one launch (start us, length us, event | category | flops | bytes accessed | tf_op | source)
XLA Modules:
  0.0 1114.2 jit_solution(7173744732596743457)
XLA Ops:
  6.5 0.0 copy-start
  6.5 1.8 stack.2
  8.3 19.3 %all-to-all-start = ((bf16[64,8,768]{2,1,0:T(8,128)(2,1)}), bf16[64,8,768]{2,1,0:T(8,128)(2,1)S(1)}, u32[]{:S(2)}, u32[]{:S(2)}) async-start(bf16[64,8,768]{2,1,0:T(8,128)(2,1)} %stack.2), calls=%async_computation | async-start | bytes 1572864 | tf_op jit(solution)/shard_map/all_to_all | solution.py:31
  27.6 0.0 all-reduce.2.cloned.1.call-start
  27.7 0.7 compare_reduce_fusion.1
  28.4 0.9 compare_reduce_fusion
  29.3 0.1 copy.39
  29.4 0.1 broadcast_bitcast_fusion
  29.5 37.9 %all-to-all-done = bf16[64,8,768]{2,1,0:T(8,128)(2,1)S(1)} async-done(((bf16[64,8,768]{2,1,0:T(8,128)(2,1)}), bf16[64,8,768]{2,1,0:T(8,128)(2,1)S(1)}, u32[]{:S(2)}, u32[]{:S(2)}) %all-to-all-start) | async-done | bytes 786464 | tf_op jit(solution)/shard_map/all_to_all | solution.py:31
  67.4 0.9 reshape.87
  68.3 0.1 broadcast_in_dim.67
  68.4 0.0 copy-start.17
  68.4 3.9 fusion
  72.3 222.5 %pmax.7 = f32[512,6]{0,1:T(8,128)S(1)} all-reduce(f32[512,6]{0,1:T(8,128)S(1)} %get-tuple-element.7), channel_id=1, replica_groups=mesh['ctx'=64,'exp'=8] {'ctx'}, use_global_device_ids=true, to_apply=%region_3.4 | all-reduce | flops 3072 | bytes 24576 | tf_op jit(solution)/shard_map/pmax | solution.py:50
  294.7 5.6 fusion.13
  300.4 0.0 all-reduce.2.cloned.1.call-update
  300.4 0.0 reduce-scatter.2.cloned.1.call-start
  300.5 4.1 convert_reduce_fusion
  304.5 0.0 copy-start.4
  304.6 0.0 copy-start.9
  304.6 0.0 copy-start.12
  304.6 0.0 copy-start.5
  304.6 0.0 copy-start.13
  304.6 219.0 %psum.29 = f32[512,6]{0,1:T(8,128)S(1)} all-reduce(f32[512,6]{0,1:T(8,128)S(1)} %convert_reduce_fusion), channel_id=1, replica_groups=mesh['ctx'=64,'exp'=8] {'ctx'}, use_global_device_ids=true, to_apply=%region_6.7 | all-reduce | flops 3072 | bytes 24576 | tf_op jit(solution)/shard_map/psum | solution.py:54
  523.6 89.1 %all-reduce.2.cloned.1.call-done = f32[512,1,6,128]{3,0,2,1:T(8,128)} async-done(((f32[512,1,6,128]{3,0,2,1:T(8,128)}), f32[512,1,6,128]{3,0,2,1:T(8,128)}) %all-reduce.2.cloned.1.call-update) | async-done | bytes 1572880 | tf_op jit(solution)/shard_map/psum | solution.py:54
  612.8 1.9 divide_convert_fusion
  614.6 0.3 copy.42
  614.9 1.1 fusion.45
  616.0 0.0 reduce-scatter.2.cloned.1.call-update
  616.1 0.0 all-gather.3.cloned.1.call-start
  616.1 0.0 copy-done.9
  616.1 0.0 copy-done.12
  616.1 0.6 compare_and_fusion
  616.7 0.6 copy-done.7
  617.3 0.7 fusion.38
  618.0 45.7 %reduce-scatter.2.cloned.1.call-done = f32[64,96]{1,0:T(8,128)} async-done(((f32[512,96]{1,0:T(8,128)}), f32[64,96]{1,0:T(8,128)}) %reduce-scatter.2.cloned.1.call-update) | async-done | bytes 24592 | tf_op jit(solution)/shard_map/reduce_scatter | solution.py:57
  663.6 0.9 multiply_reduce_fusion.1
  664.5 115.6 %psum.30 = f32[64]{0:T(128)S(1)} all-reduce(f32[64]{0:T(128)S(1)} %multiply_reduce_fusion.1), channel_id=1, replica_groups=mesh['ctx'=64,'exp'=8] {'ctx'}, use_global_device_ids=true, to_apply=%region_9.10 | all-reduce | flops 64 | bytes 512 | tf_op jit(solution)/shard_map/psum | solution.py:66
  780.1 0.8 fusion.41
  780.9 72.4 %all-gather = bf16[64,96,64]{1,2,0:T(8,128)(2,1)S(1)} all-gather(bf16[1,96,64]{1,2,0:T(8,128)(2,1)S(1)} %fusion.41), channel_id=1, replica_groups=mesh['ctx'=64,'exp'=8] {'ctx'}, dimensions={0}, use_global_device_ids=true | all-gather | bytes 798720 | tf_op jit(solution)/shard_map/all_gather | solution.py:82
  853.3 0.7 copy.45
  854.0 2.3 reshape.109
  856.3 1.8 convolution_convert_fusion
  858.2 2.1 reshape.90
  860.3 88.5 %all_to_all.15 = bf16[8,20,6144]{2,1,0:T(8,128)(2,1)S(1)} all-to-all(bf16[8,20,6144]{2,1,0:T(8,128)(2,1)} %reshape.90), channel_id=1, replica_groups=mesh['ctx'=64,'exp'=8] {'exp'}, dimensions={0} | all-to-all | bytes 3932160 | tf_op jit(solution)/shard_map/all_to_all | solution.py:87
  948.8 0.0 copy-start.14
  948.8 0.0 copy-start.18
  948.8 0.8 fusion.16
  949.6 0.6 copy-done.1
  950.2 1.4 fusion.25
  951.6 0.0 all-gather.3.cloned.1.call-update
  951.6 0.1 copy.46
  951.7 0.1 reshape.100
  951.9 0.1 copy.44
  952.0 0.2 fusion.40
  952.2 113.2 %psum.31 = f32[64,8]{0,1:T(8,128)S(1)} all-reduce(f32[64,8]{0,1:T(8,128)S(1)} %fusion.40), channel_id=1, replica_groups=mesh['ctx'=64,'exp'=8] {'ctx'}, use_global_device_ids=true, to_apply=%region_10.11 | all-reduce | flops 512 | bytes 4096 | tf_op jit(solution)/shard_map/psum | solution.py:68
  1065.5 9.4 all-gather.3.cloned.1.call-done
  1074.9 3.5 fusion.28
  1078.4 22.9 %all-to-all-start.2 = ((bf16[8,20,96]{2,1,0:T(8,128)(2,1)}), bf16[8,20,96]{2,1,0:T(8,128)(2,1)S(1)}, u32[]{:S(2)}, u32[]{:S(2)}) async-start(bf16[8,20,96]{2,1,0:T(8,128)(2,1)} %fusion.28), calls=%async_computation.3 | async-start | bytes 98304 | tf_op jit(solution)/shard_map/all_to_all | solution.py:99
  1101.3 0.1 copy.43
  1101.4 4.7 all-to-all-done.2
  1106.2 0.7 gather_fusion
  1106.9 0.2 multiply_reduce_fusion
  1107.1 0.6 add_convert_fusion
  (35 shorter events, 0.2 us)
Async XLA Ops:
  6.5 942.2 %copy-start = (bf16[1,6144,128]{2,1,0:T(8,128)(2,1)S(1)}, bf16[1,6144,128]{2,1,0:T(8,128)(2,1)}, u32[]{:S(2)}) copy-start(bf16[1,6144,128]{2,1,0:T(8,128)(2,1)} %param.25) | copy-start | bytes 4718596
  6.5 61.8 %copy-start.6 = (bf16[512,128]{1,0:T(8,128)(2,1)S(1)}, bf16[512,128]{1,0:T(8,128)(2,1)}, u32[]{:S(2)}) copy-start(bf16[512,128]{1,0:T(8,128)(2,1)} %param.16) | copy-start | bytes 393220
  8.3 59.1 %all-to-all-start = ((bf16[64,8,768]{2,1,0:T(8,128)(2,1)}), bf16[64,8,768]{2,1,0:T(8,128)(2,1)S(1)}, u32[]{:S(2)}, u32[]{:S(2)}) async-start(bf16[64,8,768]{2,1,0:T(8,128)(2,1)} %stack.2), calls=%async_computation | async-start | bytes 1572864 | tf_op jit(solution)/shard_map/all_to_all | solution.py:31
  27.6 585.2 %all-reduce.2.cloned.1.call-start = ((), (), s32[]{:S(2)}) async-start(), calls=%async_computation.4 | async-start | bytes 3145728 | tf_op jit(solution)/shard_map/psum | solution.py:54
  68.4 226.4 %copy-start.17 = (bf16[512,128]{1,0:T(8,128)(2,1)S(1)}, bf16[512,128]{1,0:T(8,128)(2,1)}, u32[]{:S(2)}) copy-start(bf16[512,128]{1,0:T(8,128)(2,1)} %param.17) | copy-start | bytes 393220
  300.4 363.2 %reduce-scatter.2.cloned.1.call-start = ((), (), s32[]{:S(2)}) async-start(), calls=%async_computation.5 | async-start | bytes 294912 | tf_op jit(solution)/shard_map/reduce_scatter | solution.py:57
  304.5 310.4 %copy-start.4 = (bf16[768,96]{0,1:T(8,128)(2,1)S(1)}, bf16[768,96]{0,1:T(8,128)(2,1)}, u32[]{:S(2)}) copy-start(bf16[768,96]{0,1:T(8,128)(2,1)} %param.20) | copy-start | bytes 442372
  304.6 311.6 %copy-start.9 = (s32[64,2]{0,1:T(2,128)S(1)}, s32[64,2]{0,1:T(2,128)}, u32[]{:S(2)}) copy-start(s32[64,2]{0,1:T(2,128)} %param.23) | copy-start | bytes 1540
  304.6 311.6 %copy-start.12 = (s32[64,2]{0,1:T(2,128)S(1)}, s32[64,2]{0,1:T(2,128)}, u32[]{:S(2)}) copy-start(s32[64,2]{0,1:T(2,128)} %param.24) | copy-start | bytes 1540
  304.6 359.0 %copy-start.5 = (bf16[64,96]{1,0:T(8,128)(2,1)S(1)}, bf16[64,96]{1,0:T(8,128)(2,1)}, u32[]{:S(2)}) copy-start(bf16[64,96]{1,0:T(8,128)(2,1)} %param.14) | copy-start | bytes 36868
  304.6 475.5 %copy-start.13 = (f32[96]{0:T(128)S(1)}, f32[96]{0:T(128)}, u32[]{:S(2)}) copy-start(f32[96]{0:T(128)} %param.21) | copy-start | bytes 1156
  616.1 458.9 %all-gather.3.cloned.1.call-start = ((), (), s32[]{:S(2)}) async-start(), calls=%async_computation.6 | async-start | bytes 3194880 | tf_op jit(solution)/shard_map/all_gather | solution.py:95
  616.7 0.6 copy-start.7
  780.1 73.9 %copy-start.15 = (f32[64]{0:T(128)}, f32[64]{0:T(128)S(1)}, u32[]{:S(2)}) copy-start(f32[64]{0:T(128)S(1)} %add_rsqrt_fusion) | copy-start | bytes 772
  948.8 1.4 copy-start.1
  948.8 2.8 copy-start.8
  948.8 3.1 copy-start.11
  948.8 3.2 copy-start.3
  948.8 3.2 copy-start.14
  948.8 3.2 copy-start.16
  948.8 3.2 copy-start.18
  950.2 115.3 %copy-start.10 = (s32[64,2]{0,1:T(2,128)S(1)}, s32[64,2]{0,1:T(2,128)}, u32[]{:S(2)}) copy-start(s32[64,2]{0,1:T(2,128)} %param.23) | copy-start | bytes 1540
  950.2 124.7 %copy-start.2 = (bf16[1,8192,96]{1,2,0:T(8,128)(2,1)S(1)}, bf16[1,8192,96]{1,2,0:T(8,128)(2,1)}, u32[]{:S(2)}) copy-start(bf16[1,8192,96]{1,2,0:T(8,128)(2,1)} %param.27) | copy-start | bytes 4718596
  1078.4 27.7 %all-to-all-start.2 = ((bf16[8,20,96]{2,1,0:T(8,128)(2,1)}), bf16[8,20,96]{2,1,0:T(8,128)(2,1)S(1)}, u32[]{:S(2)}, u32[]{:S(2)}) async-start(bf16[8,20,96]{2,1,0:T(8,128)(2,1)} %fusion.28), calls=%async_computation.3 | async-start | bytes 98304 | tf_op jit(solution)/shard_map/all_to_all | solution.py:99
Sparse Core Ops, SparseCore 0:
  300.5 312.1 all-reduce.1
  616.2 47.3 reduce-scatter.1
  951.7 123.1 all-gather.2
